TPU v7x, 256 devices: a whole 4x4x8 slice. The times are simulated.
256 devices in a mesh: dp: 4 (over z_hi, core), mp: 64 (over z_lo, x, y).
Axes of the slice: x: 4, y: 4, z: 8 (z_hi: 2, z_lo: 4; z = z_hi * 4 + z_lo), core: 2. Of those that a mesh axis runs over, the one named last changes fastest.
Arguments:
- inputs: bfloat16 [512, 6144], P(('dp', 'mp')), may hold values from -6 to 6
- out_grad: bfloat16 [512, 6144], P(('dp', 'mp')), may hold values from -1.1953125 to 1.1953125
- pre_act: bfloat16 [512, 32768], P('dp', 'mp'), may hold values from -8 to 8
- norm_gain: float32 [6144], replicated, may hold values from 0.25 to 1.75
- up_weight: bfloat16 [128, 4096, 256], P('mp'), may hold values from -0.09375 to 0.09375
- down_weight: bfloat16 [128, 256, 4096], P('mp'), may hold values from -0.09375 to 0.09375
- row_blocks: int32 [128, 16], replicated, may hold values from 0 to 23, as said below
- col_blocks: int32 [128, 16], replicated, may hold values from 0 to 23, as said below
- counts: int32 [64], replicated, may hold values from 0 to 2, as said below
Outputs:
- grad_input: bfloat16 [512, 6144], P(('dp', 'mp'))
- up_grad: bfloat16 [128, 4096, 256], P('mp', 'dp')
- down_grad: bfloat16 [128, 256, 4096], P('mp', 'dp')
Inputs may be any that keep to these rules, and one draw needn't show every extreme that they name: `row_blocks`: each row holds distinct feature blocks in increasing order. `col_blocks`: each row holds distinct feature blocks in increasing order. counts[i] + counts[i + 32] <= 2 for i < 32, and some device has 2.
All inputs are finite; a program needn't handle non-finite values.
Results may differ from a plain program's by a relative error of at most 0.013.
Values may be sent and summed in bfloat16 or wider, within the bound.
A program may use at most 128 MiB of HBM per device.

v0:
```python
import jax
import jax.numpy as jnp
from jax import lax
from jax.sharding import PartitionSpec as P

EPS = 1e-06


def normalize(inputs, norm_gain):
    widened = inputs.astype(jnp.float32)
    average = jnp.mean(widened, axis=-1, keepdims=True)
    centred = widened - average
    inv_std = lax.rsqrt(jnp.mean(centred * centred, axis=-1, keepdims=True) + EPS)
    unit_rows = centred * inv_std
    return (unit_rows, inv_std, (unit_rows * norm_gain).astype(jnp.bfloat16))


def run_block(
    active, up_block, down_block, pre_block, row_ids, col_ids, normed_blocks, grad_blocks
):
    row_total = normed_blocks.shape[0]
    block_width = up_block.shape[1]

    def run_work(unused):
        picked = jnp.take(normed_blocks, row_ids, axis=1).reshape(row_total, -1)
        seen = jnp.take(grad_blocks, col_ids, axis=1).reshape(row_total, -1)
        act_grad = jnp.dot(seen, down_block.T, preferred_element_type=jnp.float32)
        activated, pullback = jax.vjp(jax.nn.gelu, pre_block.astype(jnp.float32))
        pre_grad = pullback(act_grad)[0].astype(jnp.bfloat16)
        up_part = jnp.dot(picked.T, pre_grad, preferred_element_type=jnp.float32).astype(
            jnp.bfloat16
        )
        down_part = jnp.dot(
            activated.astype(jnp.bfloat16).T, seen, preferred_element_type=jnp.float32
        ).astype(jnp.bfloat16)
        return (pre_grad, up_part, down_part)

    def run_skip(unused):
        return (
            jnp.zeros((row_total, block_width), jnp.bfloat16),
            jnp.zeros(up_block.shape, jnp.bfloat16),
            jnp.zeros(down_block.shape, jnp.bfloat16),
        )

    return lax.cond(active, run_work, run_skip, 0)


def block_term(active, row_piece, up_block):

    def block_work(piece):
        return jnp.dot(piece, up_block.T, preferred_element_type=jnp.float32)

    def block_skip(piece):
        return jnp.zeros((piece.shape[0], up_block.shape[0]), jnp.float32)

    return lax.cond(active, block_work, block_skip, row_piece)


def local(
    inputs, out_grad, pre_act, norm_gain, up_weight, down_weight, row_blocks, col_blocks, counts
):
    unit_rows, inv_std, normed = normalize(inputs, norm_gain)
    normed_all, grad_all = (
        lax.all_gather(normed, "mp", axis=0, tiled=True),
        lax.all_gather(out_grad, "mp", axis=0, tiled=True),
    )
    row_total = normed_all.shape[0]
    features = inputs.shape[1]
    block_width = up_weight.shape[2]
    block_count = features // block_width
    slot_count = up_weight.shape[0]
    normed_blocks = normed_all.reshape(row_total, block_count, block_width)
    grad_blocks = grad_all.reshape(row_total, block_count, block_width)
    own_index = lax.axis_index("mp")
    own_count = counts[own_index]
    job_list = []
    for slot_index in range(slot_count):
        job_list.append(
            (
                slot_index < own_count,
                up_weight[slot_index],
                down_weight[slot_index],
                pre_act[:, slot_index * block_width : (slot_index + 1) * block_width],
                row_blocks[own_index * slot_count + slot_index],
                col_blocks[own_index * slot_count + slot_index],
            )
        )
    results = [
        run_block(job[0], job[1], job[2], job[3], job[4], job[5], normed_blocks, grad_blocks)
        for job in job_list
    ]
    all_ids = jnp.concatenate([job[4] for job in job_list])
    row_count = inputs.shape[0] * lax.axis_size("mp")
    pieces = []
    for job, rows_result in zip(job_list, results):
        row_piece = rows_result[0]
        pieces.append(block_term(job[0], row_piece, job[1]))
    joined = jnp.concatenate(pieces, axis=1).reshape(row_count, all_ids.shape[0], block_width)
    summed = (
        jnp.zeros((row_count, block_count, block_width), jnp.float32).at[:, all_ids].add(joined)
    )
    normed_grad = lax.psum_scatter(
        summed.reshape(row_count, features), "mp", scatter_dimension=0, tiled=True
    )
    up_parts = jnp.stack([result[1] for result in results])
    down_parts = jnp.stack([result[2] for result in results])
    up_sum, down_sum = (
        lax.psum_scatter(
            up_parts.astype(jnp.float32).astype(jnp.bfloat16), "dp", scatter_dimension=1, tiled=True
        ).astype(jnp.float32),
        lax.psum_scatter(
            down_parts.astype(jnp.float32).astype(jnp.bfloat16),
            "dp",
            scatter_dimension=1,
            tiled=True,
        ).astype(jnp.float32),
    )
    scaled = normed_grad * norm_gain
    grad_input = inv_std * (
        scaled
        - jnp.mean(scaled, axis=-1, keepdims=True)
        - unit_rows * jnp.mean(scaled * unit_rows, axis=-1, keepdims=True)
    )
    return (
        grad_input.astype(jnp.bfloat16),
        up_sum.astype(jnp.bfloat16),
        down_sum.astype(jnp.bfloat16),
    )


def solution(mesh):
    placed = (
        P(("dp", "mp"), None),
        P(("dp", "mp"), None),
        P("dp", "mp"),
        P(),
        P("mp", None, None),
        P("mp", None, None),
        P(),
        P(),
        P(),
    )
    return jax.shard_map(
        local,
        mesh=mesh,
        in_specs=placed,
        out_specs=(P(("dp", "mp"), None), P("mp", "dp", None), P("mp", "dp", None)),
        check_vma=False,
    )
```

profile of v0, /device:TPU:1, one launch (start us, length us, event | category | flops | bytes accessed | tf_op | source)
XLA Modules:
  0.0 1668.7 jit_solution(3295664205519336826)
XLA Ops:
  7.2 0.9 convert_reduce_fusion
  8.1 1.0 fusion.62
  9.1 1.5 fusion.63
  10.6 0.7 all-gather.5.cloned.1.call-update
  11.4 0.9 constant_dynamic-slice_fusion.2
  12.3 1.2 dynamic_slice.23
  15.0 303.2 %all-gather.7.cloned.1.call-done = bf16[64,2,6144]{2,1,0:T(2,128)(2,1)} async-done(((bf16[1,2,6144]{2,1,0:T(2,128)(2,1)}), bf16[64,2,6144]{2,1,0:T(2,128)(2,1)}) %all-gather.7.cloned.1.call-update) | async-done | bytes 1572880 | tf_op jit(solution)/shard_map/all_gather | solution.py:64
  318.2 4.0 reshape.154
  322.2 344.5 %all-gather.5.cloned.1.call-done = bf16[64,2,6144]{2,1,0:T(2,128)(2,1)} async-done(((bf16[1,2,6144]{2,1,0:T(2,128)(2,1)}), bf16[64,2,6144]{2,1,0:T(2,128)(2,1)}) %all-gather.5.cloned.1.call-update) | async-done | bytes 1572880 | tf_op jit(solution)/shard_map/all_gather | solution.py:65
  666.7 4.0 reshape.153
  670.6 3.1 conditional.6
  670.7 1.5 stack.32
  672.1 1.6 stack.33
  673.7 3.0 conditional.4
  673.7 1.5 stack.28
  675.2 1.5 stack.29
  677.0 1.6 conditional.5
  677.0 1.6 broadcast.121
  678.5 1.9 pad_maximum_fusion
  680.4 2.4 copy.85
  683.2 6.5 scatter_fusion
  689.8 2.4 copy.77
  692.3 4.6 pad_maximum_fusion.1
  696.9 4.6 pad_maximum_fusion.2
  701.6 0.6 copy-done.11
  702.2 0.6 dynamic-slice
  703.4 748.4 %all-reduce.3.cloned.1.call-done = f32[128,6144]{0,1:T(8,128)} async-done(((f32[128,6144]{0,1:T(8,128)}), f32[128,6144]{0,1:T(8,128)}) %all-reduce.3.cloned.1.call-update) | async-done | bytes 3145744
  1451.8 2.8 constant_dynamic-slice_fusion
  1454.6 1.2 copy.78
  1456.1 0.7 multiply_convert_fusion
  1456.8 124.0 %reduce-scatter.4.cloned.1.call-done = bf16[2,1024,256]{2,1,0:T(8,128)(2,1)} async-done(((bf16[2,4096,256]{2,1,0:T(8,128)(2,1)}), bf16[2,1024,256]{2,1,0:T(8,128)(2,1)}) %reduce-scatter.4.cloned.1.call-update) | async-done | bytes 1048592 | tf_op jit(solution)/shard_map/reduce_scatter | solution.py:108
  1580.8 81.4 %reduce-scatter.6.cloned.1.call-done = bf16[2,64,4096]{2,1,0:T(8,128)(2,1)} async-done(((bf16[2,256,4096]{2,1,0:T(8,128)(2,1)}), bf16[2,64,4096]{2,1,0:T(8,128)(2,1)}) %reduce-scatter.6.cloned.1.call-update) | async-done | bytes 1048592 | tf_op jit(solution)/shard_map/reduce_scatter | solution.py:111
  (30 shorter events, 1.5 us)
Async XLA Ops:
  7.2 311.0 %all-gather.7.cloned.1.call-start = ((), (), s32[]{:S(2)}) async-start(), calls=%async_computation.5 | async-start | bytes 1597440 | tf_op jit(solution)/shard_map/all_gather | solution.py:64
  10.6 656.1 %all-gather.5.cloned.1.call-start = ((), (), s32[]{:S(2)}) async-start(), calls=%async_computation.4 | async-start | bytes 1597440 | tf_op jit(solution)/shard_map/all_gather | solution.py:65
  11.3 1440.5 %all-reduce.3.cloned.1.call-start = ((), (), s32[]{:S(2)}) async-start(), calls=%async_computation.6 | async-start | bytes 6291456
  322.2 348.4 %copy-start.9 = (bf16[128,512]{1,0:T(8,128)(2,1)S(1)}, bf16[128,512]{1,0:T(8,128)(2,1)}, u32[]{:S(2)}) copy-start(bf16[128,512]{1,0:T(8,128)(2,1)} %param.21) | copy-start | bytes 393220
  322.2 348.4 %copy-start.10 = (s32[128,16]{0,1:T(8,128)S(1)}, s32[128,16]{0,1:T(8,128)}, u32[]{:S(2)}) copy-start(s32[128,16]{0,1:T(8,128)} %param.26) | copy-start | bytes 24580
  692.2 888.5 %reduce-scatter.4.cloned.1.call-start = ((), (), s32[]{:S(2)}) async-start(), calls=%async_computation.2 | async-start | bytes 5242880 | tf_op jit(solution)/shard_map/reduce_scatter | solution.py:108
  696.9 965.3 %reduce-scatter.6.cloned.1.call-start = ((), (), s32[]{:S(2)}) async-start(), calls=%async_computation.3 | async-start | bytes 5242880 | tf_op jit(solution)/shard_map/reduce_scatter | solution.py:111
  701.5 0.7 copy-start.11
  1454.6 1.2 copy-start.3
  1454.6 1.2 copy-start.8
Sparse Core Ops, SparseCore 0:
  10.7 307.4 all-gather.6
  320.0 346.6 all-gather.4
  692.4 759.4 all-reduce.2
  1455.3 125.4 reduce-scatter.3
  1584.0 78.1 reduce-scatter.5
where the time goes:
time: 1670 us
  waiting for transfers between devices  1600 us (96%)
  local copies, waits for them, and re-layouts  28.4 us (2%)
  other arithmetic  22 us (1%)
    unnamed x6, waiting for transfers between devices  749 us
    all_gather x1, waiting for transfers between devices, local(): lax.all_gather(out_grad, 'mp', axis=0, tiled=True)  344 us
    all_gather x1, waiting for transfers between devices, local(): lax.all_gather(normed, 'mp', axis=0, tiled=True)  303 us
    reduce_scatter x1, waiting for transfers between devices, local(): lax.psum_scatter(up_parts.astype(jnp.float32).astype(jnp.bfloat16), 'dp',...  124 us
    reduce_scatter x1, waiting for transfers between devices, local(): lax.psum_scatter(down_parts.astype(jnp.float32).astype(jnp.bfloat16), 'dp...  81.4 us
  transfers between devices with their start and end apart: 5, of which 5 were waited for; matrix products, arithmetic and copies ran while one was open for 1% of the time, Pallas kernels for 0%

commit v1 on v0

v1 whole, which is shorter than its diff:
```python
import math

import jax
import jax.numpy as jnp
from jax import lax
from jax.experimental import pallas as pl
from jax.experimental.pallas import tpu as pltpu
from jax.sharding import PartitionSpec as P

EPS = 1e-06
F32 = jnp.float32
BF16 = jnp.bfloat16
PIECES = 8
PIECE = 768
BLK = 256
SLOTS = 2
KEPT = 16
FEATURES = 6144
N_COPIES = 80


def dot(a, b, dims):
    return lax.dot_general(a, b, (dims, ((), ())), preferred_element_type=F32)


def select_rows(rows, columns, source_of):
    r = lax.broadcasted_iota(jnp.int32, (rows, columns), 0)
    c = lax.broadcasted_iota(jnp.int32, (rows, columns), 1)
    return (c == source_of(r)).astype(BF16)


def gelu_pair(z):
    a = math.sqrt(2.0 / math.pi)
    z2 = z * z
    t = jnp.tanh(a * z * (1.0 + 0.044715 * z2))
    half = 0.5 * (1.0 + t)
    slope = half + 0.5 * z * (1.0 - t * t) * (a * (1.0 + 3.0 * 0.044715 * z2))
    return z * half, slope


def kernel(
    x_ref, og_ref, pre_hbm, gain_ref, up_hbm, dn_hbm, row_ref, col_ref, cnt_ref,
    gin_ref, upg_ref, dng_ref,
    up, dn, pre, pa,
    pack, gain16, unit16, inv16,
    zraw_og, zraw_nm,
    og_own, og_sib, nm_own, nm_sib,
    acc, act, pg, pgh, pgb,
    ra, rb, fa1, fa2, fb1, fb2, ga1, ga2, gb1, gb2,
    ya, xb, ha1, ha2, hb1, hb2, ka1, ka2, kb1, kb2,
    zs, zr, pos,
    local_sem, send_sem, recv_sem,
):
    dp = lax.axis_index("dp")
    mp = lax.axis_index("mp")
    h, c = lax.div(dp, 2), lax.rem(dp, 2)
    z, x, y = lax.div(mp, 16), lax.rem(lax.div(mp, 4), 4), lax.rem(mp, 4)
    z8 = h * 4 + z
    xp, xm, xo = lax.rem(x + 1, 4), lax.rem(x + 3, 4), lax.rem(x + 2, 4)
    yp, ym, yo = lax.rem(y + 1, 4), lax.rem(y + 3, 4), lax.rem(y + 2, 4)

    def device(h=h, c=c, z=z, x=x, y=y):
        return {"dp": h * 2 + c, "mp": z * 16 + x * 4 + y}

    def z_device(at):
        return device(h=lax.div(at, 4), z=lax.rem(at, 4))

    x_plus, x_minus = device(x=xp), device(x=xm)
    y_plus, y_minus = device(y=yp), device(y=ym)
    sibling = device(c=1 - c)
    partner = device(h=1 - h)

    started = []
    count = [0]

    def send(src, dst, target):
        k = count[0]
        count[0] += 1
        copy = pltpu.make_async_remote_copy(
            src_ref=src, dst_ref=dst, send_sem=send_sem.at[k], recv_sem=recv_sem.at[k],
            device_id=target, device_id_type=pl.DeviceIdType.MESH,
        )
        copy.start()
        started.append(copy)
        return k

    def arrive(k, dst):
        pltpu.make_async_remote_copy(
            src_ref=dst, dst_ref=dst, send_sem=send_sem.at[k], recv_sem=recv_sem.at[k],
            device_id=sibling, device_id_type=pl.DeviceIdType.MESH,
        ).wait_recv()

    up_copies = [
        pltpu.make_async_copy(up_hbm.at[s], up.at[s, pl.ds(0, KEPT)], local_sem.at[s])
        for s in range(SLOTS)
    ]
    dn_copy = pltpu.make_async_copy(dn_hbm, dn, local_sem.at[2])
    pre_copy = pltpu.make_async_copy(pre_hbm, pre, local_sem.at[3])
    pre_copy.start()
    dn_copy.start()
    for copy in up_copies:
        copy.start()

    barrier = pltpu.get_barrier_semaphore()
    greeted = [z_device(lax.rem(z8 + k, 8)) for k in range(1, 8)]
    greeted += [x_plus, x_minus, y_plus, y_minus, sibling]
    for target in greeted:
        pl.semaphore_signal(
            barrier, inc=1, device_id=target, device_id_type=pl.DeviceIdType.MESH
        )

    for p in range(PIECES):
        pack[2 * p : 2 * p + 2, :] = og_ref[:, p * PIECE : (p + 1) * PIECE].astype(F32)
    zraw_og[z8] = pack[...].astype(BF16)
    for p in range(PIECES):
        pack[2 * p : 2 * p + 2, :] = x_ref[:, p * PIECE : (p + 1) * PIECE].astype(F32)
        gain16[2 * p : 2 * p + 2, :] = jnp.broadcast_to(
            gain_ref[:, p * PIECE : (p + 1) * PIECE], (2, PIECE)
        )
    first = lax.rem(lax.broadcasted_iota(jnp.int32, (16, 1), 0), 2) == 0

    def token_mean(values):
        rows = jnp.sum(values, axis=1, keepdims=True)
        total0 = jnp.sum(jnp.where(first, rows, 0.0), axis=0, keepdims=True)
        total1 = jnp.sum(jnp.where(first, 0.0, rows), axis=0, keepdims=True)
        return jnp.where(first, total0, total1) * (1.0 / FEATURES)

    widened = pack[...]
    centred = widened - token_mean(widened)
    inv_std = lax.rsqrt(token_mean(centred * centred) + EPS)
    unit_rows = centred * inv_std
    unit16[...] = unit_rows
    inv16[...] = jnp.broadcast_to(inv_std, (16, 128))
    zraw_nm[z8] = (unit_rows * gain16[...]).astype(BF16)

    pl.semaphore_wait(barrier, len(greeted))

    def z_send(raw):
        return [
            (k, send(raw.at[z8], raw.at[z8], z_device(lax.rem(z8 + k, 8)))) for k in range(1, 8)
        ]

    og_z = z_send(zraw_og)
    nm_z = z_send(zraw_nm)

    pre_copy.wait()
    order = select_rows(
        128, 128, lambda r: lax.div(lax.rem(r, 8), 2) * 32 + lax.div(r, 8) * 2 + lax.rem(r, 2)
    )
    pa[0, h] = dot(order, pre[...], ((1,), (0,))).astype(BF16)
    pa_sib = send(pa.at[0, h], pa.at[1, h], sibling)
    pa_part = send(pa.at[0, h], pa.at[0, h], partner)

    def place(raw, gathered, arrivals):
        for k, sem in arrivals:
            arrive(sem, raw.at[lax.rem(z8 + 8 - k, 8)])
        order = select_rows(
            128, 128, lambda r: lax.div(lax.rem(r, 16), 2) * 16 + lax.div(r, 16) * 2 + lax.rem(r, 2)
        )
        tiles = dot(order, raw[...].reshape(128, PIECE), ((1,), (0,))).astype(BF16)
        for p in range(PIECES):
            for q in range(PIECE // 128):
                gathered[p * 6 + q, x, y] = tiles[16 * p : 16 * p + 16, 128 * q : 128 * q + 128]

    lo, lo1, lo2 = pl.ds(0, 24), pl.ds(0, 12), pl.ds(12, 12)
    hi, hi1, hi2 = pl.ds(24, 24), pl.ds(24, 12), pl.ds(36, 12)

    def ring_a(g, lane, at):
        return g.at[lane, at, y]

    def ring_b(g, lane, at):
        return g.at[lane, x, at]

    def wide_a(g, lane, at):
        return g.at[lane, :, at]

    def wide_b(g, lane, at):
        return g.at[lane, at]

    def spread(view, g, lane, at, plus, minus):
        mine = view(g, lane, at)
        return send(mine, mine, plus), send(mine, mine, minus)

    def relay(view, g, lanes, sems, at_p, at_m, plus, minus):
        lane, lane1, lane2 = lanes
        arrive(sems[0], view(g, lane, at_m))
        one = send(view(g, lane1, at_m), view(g, lane1, at_m), plus)
        arrive(sems[1], view(g, lane, at_p))
        two = send(view(g, lane2, at_p), view(g, lane2, at_p), minus)
        return one, two

    def finish(view, g, lanes, sems, at_o):
        arrive(sems[0], view(g, lanes[1], at_o))
        arrive(sems[1], view(g, lanes[2], at_o))

    lanes_a, lanes_b = (lo, lo1, lo2), (hi, hi1, hi2)

    def narrow_spread(g):
        return (
            spread(ring_a, g, lo, x, x_plus, x_minus),
            spread(ring_b, g, hi, y, y_plus, y_minus),
        )

    def narrow_relay(g, sems):
        return (
            relay(ring_a, g, lanes_a, sems[0], xp, xm, x_plus, x_minus),
            relay(ring_b, g, lanes_b, sems[1], yp, ym, y_plus, y_minus),
        )

    def narrow_finish(g, sems):
        finish(ring_a, g, lanes_a, sems[0], xo)
        finish(ring_b, g, lanes_b, sems[1], yo)

    def wide_spread(g):
        return (
            spread(wide_a, g, lo, y, y_plus, y_minus),
            spread(wide_b, g, hi, x, x_plus, x_minus),
        )

    def wide_relay(g, sems):
        return (
            relay(wide_a, g, lanes_a, sems[0], yp, ym, y_plus, y_minus),
            relay(wide_b, g, lanes_b, sems[1], xp, xm, x_plus, x_minus),
        )

    def wide_finish(g, sems):
        finish(wide_a, g, lanes_a, sems[0], yo)
        finish(wide_b, g, lanes_b, sems[1], xo)

    place(zraw_og, og_own, og_z)
    og_n1 = narrow_spread(og_own)
    place(zraw_nm, nm_own, nm_z)
    nm_n1 = narrow_spread(nm_own)
    og_n2 = narrow_relay(og_own, og_n1)
    nm_n2 = narrow_relay(nm_own, nm_n1)

    for s in range(SLOTS):
        up[s, KEPT] = jnp.zeros((BLK, BLK), BF16)

    def locate(b, carry):
        for s in range(SLOTS):
            found = jnp.int32(KEPT)
            for k in range(KEPT):
                found = jnp.where(row_ref[2 * mp + s, k] == b, k, found)
            pos[s * 24 + b] = found
        return carry

    narrow_finish(og_own, og_n2)
    og_w1 = wide_spread(og_own)
    lax.fori_loop(0, 24, locate, 0)
    arrive(pa_part, pa.at[0, 1 - h])
    pa_fwd = send(pa.at[0, 1 - h], pa.at[1, 1 - h], sibling)
    narrow_finish(nm_own, nm_n2)
    og_w2 = wide_relay(og_own, og_w1)
    nm_w1 = wide_spread(nm_own)
    dn_copy.wait()
    for copy in up_copies:
        copy.wait()
    wide_finish(og_own, og_w2)
    og_s = send(og_own, og_sib, sibling)

    live = [s < cnt_ref[mp] for s in range(SLOTS)]

    def tokens(g, b):
        return jnp.concatenate([g[2 * b], g[2 * b + 1]], axis=-1).reshape(BLK, BLK)

    def back(g, group):
        for s in range(SLOTS):

            def grow(k, carry):
                parts = [tokens(g, col_ref[2 * mp + s, 4 * k + j]) for j in range(4)]
                start = pl.multiple_of(k * 1024, 1024)
                term = dot(
                    jnp.concatenate(parts, axis=1), dn[s, :, pl.ds(start, 1024)], ((1,), (1,))
                )

                @pl.when(k == 0)
                def _():
                    acc[s] = term

                @pl.when(k > 0)
                def _():
                    acc[s] += term

                return carry

            lax.fori_loop(0, KEPT // 4, grow, 0)
        mine = h == 0

        def derive(j, carry):
            at32 = pl.multiple_of(j * 32, 32)
            at16 = pl.multiple_of(j * 16, 16)
            rows32 = pl.multiple_of(group * 256 + j * 32, 32)
            for s in range(SLOTS):
                lanes = slice(s * BLK, (s + 1) * BLK)
                grads = acc[s, pl.ds(at32, 32), :].reshape(2, 2, 8, BLK)
                kept, acts = [], []
                for half in range(2):
                    value, slope = gelu_pair(pa[group, half, pl.ds(at16, 16), lanes].astype(F32))
                    grad = grads[:, half].reshape(16, BLK) * slope
                    kept.append(jnp.where(live[s], grad, 0.0))
                    acts.append(jnp.where(live[s], value, 0.0).reshape(2, 8, BLK))
                if group == 0:
                    pgh[pl.ds(at16, 16), lanes] = jnp.where(mine, kept[0], kept[1]).astype(BF16)
                kept = [part.reshape(2, 8, BLK) for part in kept]
                pg[pl.ds(rows32, 32), lanes] = jnp.stack(kept, 1).reshape(32, BLK).astype(BF16)
                act[pl.ds(rows32, 32), lanes] = jnp.stack(acts, 1).reshape(32, BLK).astype(BF16)
            return carry

        lax.fori_loop(0, 8, derive, 0)

    back(og_own, 0)

    order = select_rows(
        128, 128, lambda r: lax.div(lax.rem(r, 32), 8) * 32 + lax.div(r, 32) * 8 + lax.rem(r, 8)
    )
    pgb[...] = dot(order, pgh[...], ((1,), (0,))).astype(BF16)

    def terms(source, out, base):
        def one(b, carry):
            weights = [up[s, pos[s * 24 + base + b]] for s in range(SLOTS)]
            term = dot(source[...], jnp.concatenate(weights, axis=1), ((1,), (1,))).astype(BF16)
            for q in range(4):
                out[q, b] = term[32 * q : 32 * q + 32]
            return carry

        lax.fori_loop(0, 12, one, 0)

    def reduce_start(r, half, at_o, f1, f2, plus, minus):
        n = half * 2
        return (
            send(r.at[at_o, pl.ds(0, half)], f1, plus),
            send(r.at[at_o, pl.ds(half, n - half)], f2, minus),
        )

    def reduce_relay(r, half, sems, at_p, at_m, f1, f2, g1, g2, plus, minus):
        arrive(sems[0], f1)
        for j in range(half):
            r[at_p, j] = (r[at_p, j].astype(F32) + f1[j].astype(F32)).astype(BF16)
        one = send(r.at[at_p], g1, plus)
        arrive(sems[1], f2)
        for j in range(half):
            r[at_m, half + j] = (r[at_m, half + j].astype(F32) + f2[j].astype(F32)).astype(BF16)
        two = send(r.at[at_m], g2, minus)
        return one, two

    def repack(r, sems, at, g1, g2, out):
        arrive(sems[0], g1)
        arrive(sems[1], g2)
        for j in range(6):
            top, low = [
                r[at, b].astype(F32) + g1[b].astype(F32) + g2[b].astype(F32) for b in (j, 6 + j)
            ]
            for q in range(4):
                rows = slice(8 * q, 8 * q + 8)
                out[q, j] = jnp.concatenate([top[rows], low[rows]], axis=0).astype(BF16)

    terms(pgh, ra, 0)
    a1 = reduce_start(ra, 6, xo, fa1, fa2, x_plus, x_minus)
    terms(pgb, rb, 12)
    b1 = reduce_start(rb, 6, yo, fb1, fb2, y_plus, y_minus)
    nm_w2 = wide_relay(nm_own, nm_w1)
    a2 = reduce_relay(ra, 6, a1, xp, xm, fa1, fa2, ga1, ga2, x_plus, x_minus)
    b2 = reduce_relay(rb, 6, b1, yp, ym, fb1, fb2, gb1, gb2, y_plus, y_minus)

    arrive(pa_sib, pa.at[1, h])
    arrive(pa_fwd, pa.at[1, 1 - h])
    arrive(og_s, og_sib)
    back(og_sib, 1)

    repack(ra, a2, x, ga1, ga2, ya)
    a3 = reduce_start(ya, 3, yo, ha1, ha2, y_plus, y_minus)
    repack(rb, b2, y, gb1, gb2, xb)
    b3 = reduce_start(xb, 3, xo, hb1, hb2, x_plus, x_minus)
    wide_finish(nm_own, nm_w2)
    nm_s = send(nm_own, nm_sib, sibling)

    def down(s):
        lanes = slice(s * BLK, (s + 1) * BLK)
        pick = select_rows(64, BLK, lambda r: r + dp * 64)
        mine = dot(pick, act[:, lanes], ((1,), (1,))).astype(BF16)

        def one(k, carry):
            b = col_ref[2 * mp + s, k]
            seen = jnp.concatenate([tokens(og_own, b), tokens(og_sib, b)], axis=0)
            start = pl.multiple_of(k * BLK, BLK)
            dng_ref[s, :, pl.ds(start, BLK)] = dot(mine, seen, ((1,), (0,))).astype(BF16)
            return carry

        lax.fori_loop(0, KEPT, one, 0)

    a4 = reduce_relay(ya, 3, a3, yp, ym, ha1, ha2, ka1, ka2, y_plus, y_minus)
    b4 = reduce_relay(xb, 3, b3, xp, xm, hb1, hb2, kb1, kb2, x_plus, x_minus)
    down(0)

    def total(r, sems, at, g1, g2):
        arrive(sems[0], g1)
        arrive(sems[1], g2)
        sums = [r[at, j].astype(F32) + g1[j].astype(F32) + g2[j].astype(F32) for j in range(6)]
        return [
            jnp.concatenate(sums[3 * q : 3 * q + 3], axis=1).astype(BF16) for q in range(2)
        ]

    stacked = jnp.concatenate(total(ya, a4, y, ka1, ka2) + total(xb, b4, x, kb1, kb2), axis=0)
    order = select_rows(
        64,
        64,
        lambda r: lax.div(lax.rem(r, 16), 8) * 32
        + lax.rem(lax.div(r, 2), 2) * 16
        + lax.rem(lax.div(r, 4), 2) * 8
        + lax.div(r, 16) * 2
        + lax.rem(r, 2),
    )
    zs[...] = dot(order, stacked, ((1,), (0,))).astype(BF16).reshape(4, 16, PIECE)
    z_last = []
    for k in range(1, 4):
        to = lax.rem(z + k, 4)
        z_last.append(send(zs.at[to], zr.at[k - 1], device(z=to)))

    down(1)

    for k in range(3):
        arrive(z_last[k], zr.at[k])
    normed_grad = (
        zs[z].astype(F32) + zr[0].astype(F32) + zr[1].astype(F32) + zr[2].astype(F32)
    )
    scaled = normed_grad * gain16[...]
    unit_rows = unit16[...]
    pack[...] = inv16[:, 0:1] * (
        scaled - token_mean(scaled) - unit_rows * token_mean(scaled * unit_rows)
    )
    for p in range(PIECES):
        gin_ref[:, p * PIECE : (p + 1) * PIECE] = pack[2 * p : 2 * p + 2, :].astype(BF16)

    arrive(nm_s, nm_sib)

    for s in range(SLOTS):
        lanes = slice(s * BLK, (s + 1) * BLK)

        def grow_up(k, carry):
            b = row_ref[2 * mp + s, dp * 4 + k]
            picked = jnp.concatenate([tokens(nm_own, b), tokens(nm_sib, b)], axis=0)
            start = pl.multiple_of(k * BLK, BLK)
            upg_ref[s, pl.ds(start, BLK), :] = dot(picked, pg[:, lanes], ((0,), (0,))).astype(BF16)
            return carry

        lax.fori_loop(0, 4, grow_up, 0)

    for copy in started:
        copy.wait_send()


def local(
    inputs, out_grad, pre_act, norm_gain, up_weight, down_weight, row_blocks, col_blocks, counts
):
    vmem = pl.BlockSpec(memory_space=pltpu.VMEM)
    smem = pl.BlockSpec(memory_space=pltpu.SMEM)
    hbm = pl.BlockSpec(memory_space=pl.ANY)
    gathered = pltpu.VMEM((48, 4, 4, 16, 128), BF16)
    return pl.pallas_call(
        kernel,
        out_shape=(
            jax.ShapeDtypeStruct((2, FEATURES), BF16),
            jax.ShapeDtypeStruct((SLOTS, 1024, BLK), BF16),
            jax.ShapeDtypeStruct((SLOTS, 64, 4096), BF16),
        ),
        in_specs=[vmem, vmem, hbm, vmem, hbm, hbm, smem, smem, smem],
        out_specs=(vmem, vmem, vmem),
        scratch_shapes=[
            pltpu.VMEM((SLOTS, KEPT + 1, BLK, BLK), BF16),
            pltpu.VMEM((SLOTS, BLK, 4096), BF16),
            pltpu.VMEM((128, 512), BF16),
            pltpu.VMEM((2, 2, 128, 512), BF16),
            pltpu.VMEM((16, PIECE), F32),
            pltpu.VMEM((16, PIECE), F32),
            pltpu.VMEM((16, PIECE), F32),
            pltpu.VMEM((16, 128), F32),
            pltpu.VMEM((8, 16, PIECE), BF16),
            pltpu.VMEM((8, 16, PIECE), BF16),
            gathered, gathered, gathered, gathered,
            pltpu.VMEM((SLOTS, 256, BLK), F32),
            pltpu.VMEM((512, 512), BF16),
            pltpu.VMEM((512, 512), BF16),
            pltpu.VMEM((128, 512), BF16),
            pltpu.VMEM((128, 512), BF16),
        ]
        + [pltpu.VMEM((4, 12, 32, BLK), BF16)] * 2
        + [pltpu.VMEM((6, 32, BLK), BF16)] * 4
        + [pltpu.VMEM((12, 32, BLK), BF16)] * 4
        + [pltpu.VMEM((4, 6, 16, BLK), BF16)] * 2
        + [pltpu.VMEM((3, 16, BLK), BF16)] * 4
        + [pltpu.VMEM((6, 16, BLK), BF16)] * 4
        + [
            pltpu.VMEM((4, 16, PIECE), BF16),
            pltpu.VMEM((3, 16, PIECE), BF16),
            pltpu.SMEM((48,), jnp.int32),
            pltpu.SemaphoreType.DMA((4,)),
            pltpu.SemaphoreType.DMA((N_COPIES,)),
            pltpu.SemaphoreType.DMA((N_COPIES,)),
        ],
        compiler_params=pltpu.CompilerParams(
            collective_id=0, has_side_effects=True, vmem_limit_bytes=48 * 1024 * 1024
        ),
    )(
        inputs,
        out_grad,
        pre_act,
        norm_gain.reshape(1, FEATURES),
        up_weight.reshape(SLOTS, KEPT, BLK, BLK),
        down_weight,
        row_blocks,
        col_blocks,
        counts,
    )


def solution(mesh):
    placed = (
        P(("dp", "mp"), None),
        P(("dp", "mp"), None),
        P("dp", "mp"),
        P(),
        P("mp", None, None),
        P("mp", None, None),
        P(),
        P(),
        P(),
    )
    return jax.shard_map(
        local,
        mesh=mesh,
        in_specs=placed,
        out_specs=(P(("dp", "mp"), None), P("mp", "dp", None), P("mp", "dp", None)),
        check_vma=False,
    )
```

time: 1670 us -> 93.4 us (0.06)
  the two profiles are of different devices: /device:TPU:1 before, /device:TPU:2 now
where the time goes in v1:
time: 93.4 us; the launch traced here: 93 us
  Pallas kernels  84.5 us (90%)
  local copies, waits for them, and re-layouts  7.91 us (8%)
    pallas_call x1, Pallas kernels, local(): pl.pallas_call(kernel, out_shape=(jax.ShapeDtypeStruct((2, FEATURES), BF1...  84.5 us
    unnamed x15, local copies, waits for them, and re-layouts  7.91 us

profile of v1, /device:TPU:2, one launch (start us, length us, event | category | flops | bytes accessed | tf_op | source)
XLA Modules:
  0.0 93.0 jit_solution(16221370600507576818)
XLA Ops:
  0.6 0.8 copy.12.row_ref
  1.4 0.8 copy.13.col_ref
  2.2 0.0 copy-start
  2.2 0.9 copy-done
  3.1 0.0 copy-start.1
  3.1 0.7 copy-done.1
  3.9 0.0 copy-start.2
  3.9 0.7 copy-done.2
  4.6 0.0 copy-start.3
  4.6 0.7 copy-done.3
  5.3 0.0 copy-start.4
  5.3 0.7 copy-done.4
  6.0 84.5 %shard_map.112 = (bf16[2,6144]{1,0:T(2,128)(2,1)S(1)}, bf16[2,1024,256]{2,1,0:T(8,128)(2,1)S(1)}, bf16[2,64,4096]{2,1,0:T(8,128)(2,1)S(1)}) custom-call(bf16[2,6144]{1,0:T(2,128)(2,1)S(1)} %copy-done.1, bf16[2,6144]{1,0:T(2,128)(2,1)S(1)} %copy-done.2, bf16[128,512]{1,0:T(8,128)(2,1)S(1)} %copy-done, f32[1,6144]{1,0:T(1,128)S(1)} %bitcast.2, ...), custom_call_target="tpu_custom_call" | custom-call | tf_op jit(solution)/shard_map/pallas_call | solution.py:460
  90.5 0.6 copy.17
  91.1 1.0 %copy.18 = bf16[2,1024,256]{2,1,0:T(8,128)(2,1)} copy(bf16[2,1024,256]{2,1,0:T(8,128)(2,1)S(1)} %get-tuple-element.7) | data formatting | bytes 2097152
  92.1 1.0 %copy.19 = bf16[2,64,4096]{2,1,0:T(8,128)(2,1)} copy(bf16[2,64,4096]{2,1,0:T(8,128)(2,1)S(1)} %get-tuple-element.8) | data formatting | bytes 2097152
Async XLA Ops:
  2.2 0.9 copy-start
  3.1 0.7 copy-start.1
  3.9 0.7 copy-start.2
  4.6 0.7 copy-start.3
  5.3 0.7 copy-start.4

commit v2 on v1

v2 whole, which is shorter than its diff:
```python
import math

import jax
import jax.numpy as jnp
from jax import lax
from jax.experimental import pallas as pl
from jax.experimental.pallas import tpu as pltpu
from jax.sharding import PartitionSpec as P

EPS = 1e-06
F32 = jnp.float32
BF16 = jnp.bfloat16
PIECES = 8
PIECE = 768
BLK = 256
SLOTS = 2
KEPT = 16
FEATURES = 6144
LANES = 24
N_COPIES = 112


def dot(a, b, dims):
    return lax.dot_general(a, b, (dims, ((), ())), preferred_element_type=F32)


def select_rows(rows, columns, source_of):
    r = lax.broadcasted_iota(jnp.int32, (rows, columns), 0)
    c = lax.broadcasted_iota(jnp.int32, (rows, columns), 1)
    return (c == source_of(r)).astype(BF16)


def gelu_pair(z):
    a = math.sqrt(2.0 / math.pi)
    z2 = z * z
    t = jnp.tanh(a * z * (1.0 + 0.044715 * z2))
    half = 0.5 * (1.0 + t)
    slope = half + 0.5 * z * (1.0 - t * t) * (a * (1.0 + 3.0 * 0.044715 * z2))
    return z * half, slope


def kernel(
    x_hbm, og_hbm, pre_hbm, gain_hbm, up_hbm, dn_hbm, row_ref, col_ref, cnt_ref,
    gin_ref, upg_ref, dng_ref,
    x_ref, og_ref, gain_ref, up, dn, pre, pa,
    pack, gain16, unit16, inv16,
    raw_own, raw_oth, raw_nm,
    o_own, o_oth, t0, t1, t2, t3, n_own, n_sib,
    acc, act, pg, pg_z, pgb,
    ra, rb, ga, gb, ya, xb, ka, kb,
    zs, zr, pos,
    local_sem, send_sem, recv_sem,
):
    dp = lax.axis_index("dp")
    mp = lax.axis_index("mp")
    h, c = lax.div(dp, 2), lax.rem(dp, 2)
    z, x, y = lax.div(mp, 16), lax.rem(lax.div(mp, 4), 4), lax.rem(mp, 4)
    z8 = h * 4 + z

    def device(h=h, c=c, z=z, x=x, y=y):
        return {"dp": h * 2 + c, "mp": z * 16 + x * 4 + y}

    def around(at, by, n=4):
        return lax.rem(at + by + n, n)

    def z_device(at):
        return device(h=lax.div(at, 4), z=lax.rem(at, 4))

    x_peer = {d: device(x=around(x, d)) for d in (1, 2, 3)}
    y_peer = {d: device(y=around(y, d)) for d in (1, 2, 3)}
    z_plus, z_minus = z_device(around(z8, 1, 8)), z_device(around(z8, -1, 8))
    sibling = device(c=1 - c)
    partner = device(h=1 - h)

    started = []
    count = [0]

    def send(src, dst, target):
        k = count[0]
        count[0] += 1
        copy = pltpu.make_async_remote_copy(
            src_ref=src, dst_ref=dst, send_sem=send_sem.at[k], recv_sem=recv_sem.at[k],
            device_id=target, device_id_type=pl.DeviceIdType.MESH,
        )
        copy.start()
        started.append(copy)
        return k

    def arrive(k, dst):
        pltpu.make_async_remote_copy(
            src_ref=dst, dst_ref=dst, send_sem=send_sem.at[k], recv_sem=recv_sem.at[k],
            device_id=sibling, device_id_type=pl.DeviceIdType.MESH,
        ).wait_recv()

    def fetch(src, dst, k):
        copy = pltpu.make_async_copy(src, dst, local_sem.at[k])
        copy.start()
        return copy

    og_copy = fetch(og_hbm, og_ref, 0)
    x_copy = fetch(x_hbm, x_ref, 1)
    gain_copy = fetch(gain_hbm, gain_ref, 2)
    pre_copy = fetch(pre_hbm, pre, 3)

    barrier = pltpu.get_barrier_semaphore()
    greeted = [z_device(around(z8, k, 8)) for k in range(1, 8)]
    greeted += list(x_peer.values()) + list(y_peer.values()) + [sibling]
    for target in greeted:
        pl.semaphore_signal(
            barrier, inc=1, device_id=target, device_id_type=pl.DeviceIdType.MESH
        )

    weight_copies = [fetch(dn_hbm, dn, 4)]
    weight_copies += [fetch(up_hbm.at[s], up.at[s, pl.ds(0, KEPT)], 5 + s) for s in range(SLOTS)]

    og_copy.wait()
    for p in range(PIECES):
        pack[2 * p : 2 * p + 2, :] = og_ref[:, p * PIECE : (p + 1) * PIECE].astype(F32)
    raw_own[z] = pack[...].astype(BF16)
    x_copy.wait()
    gain_copy.wait()
    for p in range(PIECES):
        pack[2 * p : 2 * p + 2, :] = x_ref[:, p * PIECE : (p + 1) * PIECE].astype(F32)
        gain16[2 * p : 2 * p + 2, :] = jnp.broadcast_to(
            gain_ref[:, p * PIECE : (p + 1) * PIECE], (2, PIECE)
        )
    first = lax.rem(lax.broadcasted_iota(jnp.int32, (16, 1), 0), 2) == 0

    def token_mean(values):
        rows = jnp.sum(values, axis=1, keepdims=True)
        total0 = jnp.sum(jnp.where(first, rows, 0.0), axis=0, keepdims=True)
        total1 = jnp.sum(jnp.where(first, 0.0, rows), axis=0, keepdims=True)
        return jnp.where(first, total0, total1) * (1.0 / FEATURES)

    widened = pack[...]
    centred = widened - token_mean(widened)
    inv_std = lax.rsqrt(token_mean(centred * centred) + EPS)
    unit_rows = centred * inv_std
    unit16[...] = unit_rows
    inv16[...] = jnp.broadcast_to(inv_std, (16, 128))
    raw_nm[y, x] = (unit_rows * gain16[...]).astype(BF16)

    pl.semaphore_wait(barrier, len(greeted))

    own_z = [
        (d, send(raw_own.at[z], raw_own.at[z], device(z=around(z, d)))) for d in (1, 2, 3)
    ]
    nm_x = [(d, send(raw_nm.at[y, x], raw_nm.at[y, x], x_peer[d])) for d in (1, 2, 3)]
    oth_z = [
        (d, send(raw_own.at[z], raw_oth.at[z], device(h=1 - h, z=around(z, d)))) for d in range(4)
    ]

    pre_copy.wait()
    order = select_rows(
        128, 128, lambda r: lax.div(lax.rem(r, 8), 2) * 32 + lax.div(r, 8) * 2 + lax.rem(r, 2)
    )
    pa[0] = dot(order, pre[...], ((1,), (0,))).astype(BF16)
    pa_sib = send(pa.at[0], pa.at[2], sibling)

    def place(raw, tiles, arrivals):
        for d, sem in arrivals:
            arrive(sem, raw.at[around(z, -d)])
        order = select_rows(
            64,
            64,
            lambda r: lax.div(lax.rem(r, 8), 2) * 16
            + lax.div(lax.rem(r, 16), 8) * 8
            + lax.div(r, 16) * 2
            + lax.rem(r, 2),
        )
        out = dot(order, raw[...].reshape(64, PIECE), ((1,), (0,))).astype(BF16)
        for p in range(4):
            for q in range(6):
                tiles[p * 6 + q, x, y] = out[16 * p : 16 * p + 16, 128 * q : 128 * q + 128]

    lane_a, lane_b = pl.ds(0, 12), pl.ds(12, 12)

    def narrow_send(o):
        a, b = o.at[lane_a, x, y], o.at[lane_b, x, y]
        return [(d, send(a, a, x_peer[d]), send(b, b, y_peer[d])) for d in (1, 3, 2)]

    def column_send(o, at_x, at_y):
        a, b = o.at[lane_a, at_x, y], o.at[lane_b, x, at_y]
        return [(d, send(a, a, y_peer[d]), send(b, b, x_peer[d])) for d in (1, 3, 2)]

    def narrow_wait(o, sem):
        d, sem_a, sem_b = sem
        arrive(sem_a, o.at[lane_a, around(x, -d), y])
        arrive(sem_b, o.at[lane_b, x, around(y, -d)])

    place(raw_own, o_own, own_z)
    own_n = narrow_send(o_own)
    own_w = [(0, column_send(o_own, x, y))]
    pa_part = send(pa.at[0], pa.at[1], partner)
    for d, sem in nm_x:
        arrive(sem, raw_nm.at[y, around(x, -d)])
    nm_y = [(d, send(raw_nm.at[y], raw_nm.at[y], y_peer[d])) for d in (1, 2, 3)]
    place(raw_oth, o_oth, oth_z)
    for sem in own_n:
        narrow_wait(o_own, sem)
        own_w.append((sem[0], column_send(o_own, around(x, -sem[0]), around(y, -sem[0]))))
    oth_n = narrow_send(o_oth)

    for d, sem in nm_y:
        arrive(sem, raw_nm.at[around(y, -d)])
    order = select_rows(
        256,
        256,
        lambda r: lax.div(lax.rem(r, 8), 2) * 64
        + lax.div(lax.rem(r, 32), 8) * 16
        + lax.div(r, 32) * 2
        + lax.rem(r, 2),
    )
    out = dot(order, raw_nm[...].reshape(256, PIECE), ((1,), (0,))).astype(BF16)
    for p in range(PIECES):
        for q in range(6):
            n_own[z8, p * 6 + q] = out[32 * p : 32 * p + 32, 128 * q : 128 * q + 128]

    steps = [(0, 0), (0, 1), (1, 0), (1, 1), (2, 0), (2, 1), (3, 0)]
    halves = (pl.ds(0, 24), pl.ds(24, 24))
    nm_sems = {}

    def ring_send(n):
        far, half = steps[n]
        plus = n_own.at[around(z8, -far, 8), halves[half]]
        minus = n_own.at[around(z8, far, 8), halves[1 - half]]
        nm_sems[n] = (send(plus, plus, z_plus), send(minus, minus, z_minus))

    nm_sib = []

    def to_sibling(at):
        nm_sib.append((at, send(n_own.at[at], n_sib.at[at], sibling)))

    def ring_poll(n):
        far, half = steps[n]
        arrive(nm_sems[n][0], n_own.at[around(z8, -far - 1, 8), halves[half]])
        arrive(nm_sems[n][1], n_own.at[around(z8, far + 1, 8), halves[1 - half]])
        if n + 2 < len(steps):
            ring_send(n + 2)
        if half == 1:
            to_sibling(around(z8, far + 1, 8))
            to_sibling(around(z8, -far - 1, 8))
        if n == 6:
            to_sibling(around(z8, 4, 8))

    ring_send(0)
    ring_send(1)
    to_sibling(z8)

    for s in range(SLOTS):
        up[s, KEPT] = jnp.zeros((BLK, BLK), BF16)

    def locate(b, carry):
        for s in range(SLOTS):
            found = jnp.int32(KEPT)
            for k in range(KEPT):
                found = jnp.where(row_ref[k, 2 * mp + s] == b, k, found)
            pos[s * 24 + b] = found
        return carry

    lax.fori_loop(0, 24, locate, 0)
    for sem in oth_n:
        narrow_wait(o_oth, sem)
    arrive(pa_part, pa.at[1])
    pa_fwd = send(pa.at[1], pa.at[3], sibling)
    for copy in weight_copies:
        copy.wait()
    ring_poll(0)
    for far, sems in own_w:
        for d, sem_a, sem_b in sems:
            arrive(sem_a, o_own.at[lane_a, around(x, -far), around(y, -d)])
            arrive(sem_b, o_own.at[lane_b, around(x, -d), around(y, -far)])
    a, b = o_oth.at[lane_a, :, y], o_oth.at[lane_b, x]
    oth_w = [(d, send(a, a, y_peer[d]), send(b, b, x_peer[d])) for d in (1, 3, 2)]

    def unpack(o, t):
        def one(k, carry):
            rows = o[k].astype(F32).reshape(16, 2, 8, 128)
            t[k] = rows[:, 0].reshape(128, 128).astype(BF16)
            t[LANES + k] = rows[:, 1].reshape(128, 128).astype(BF16)
            return carry

        lax.fori_loop(0, LANES, one, 0)

    unpack(o_own, t0)
    t_sib0 = send(t0, t2, sibling)

    live = [s < cnt_ref[mp] for s in range(SLOTS)]

    def tokens(t, b):
        return jnp.concatenate([t[2 * b], t[2 * b + 1]], axis=-1)

    def back(groups):
        rows = 128 * len(groups)
        for s in range(SLOTS):

            def grow(k, carry):
                parts = []
                for j in range(4):
                    b = col_ref[4 * k + j, 2 * mp + s]
                    parts.append(jnp.concatenate([tokens(t, b) for t in groups.values()], axis=0))
                start = pl.multiple_of(k * 1024, 1024)
                term = dot(
                    jnp.concatenate(parts, axis=1), dn[s, :, pl.ds(start, 1024)], ((1,), (1,))
                )

                @pl.when(k == 0)
                def _():
                    acc[s, 0:rows] = term

                @pl.when(k > 0)
                def _():
                    acc[s, 0:rows] += term

                return carry

            lax.fori_loop(0, KEPT // 4, grow, 0)

        def derive(j, carry):
            at = pl.ds(pl.multiple_of(j * 16, 16), 16)
            for n, g in enumerate(groups):
                for s in range(SLOTS):
                    lanes = slice(s * BLK, (s + 1) * BLK)
                    value, slope = gelu_pair(pa[g, at, lanes].astype(F32))
                    grad = acc[s, pl.ds(pl.multiple_of(n * 128 + j * 16, 16), 16), :] * slope
                    pg[g, at, lanes] = jnp.where(live[s], grad, 0.0).astype(BF16)
                    act[g, at, lanes] = jnp.where(live[s], value, 0.0).astype(BF16)
            return carry

        lax.fori_loop(0, 8, derive, 0)

    back({0: t0})

    order = select_rows(
        128, 128, lambda r: lax.div(lax.rem(r, 32), 8) * 32 + lax.div(r, 32) * 8 + lax.rem(r, 8)
    )
    pgb[...] = dot(order, pg[0], ((1,), (0,))).astype(BF16)

    def terms(source, out, base, first):
        def one(b, carry):
            weights = [up[s, pos[s * 24 + base + b]] for s in range(SLOTS)]
            term = dot(source, jnp.concatenate(weights, axis=1), ((1,), (1,))).astype(BF16)
            for q in range(4):
                out[q, b] = term[32 * q : 32 * q + 32]
            return carry

        lax.fori_loop(first, first + 6, one, 0)

    def reduce_send(r, at, g, peers, blocks):
        return [
            (d, send(r.at[around(at, d), blocks], g.at[d - 1, blocks], peers[d])) for d in (2, 1, 3)
        ]

    part0, part1 = pl.ds(0, 6), pl.ds(6, 6)
    terms(pg[0], ra, 0, 0)
    a1 = reduce_send(ra, x, ga, x_peer, part0)
    terms(pgb[...], rb, 12, 0)
    b1 = reduce_send(rb, y, gb, y_peer, part0)
    terms(pg[0], ra, 0, 6)
    a2 = reduce_send(ra, x, ga, x_peer, part1)
    terms(pgb[...], rb, 12, 6)
    b2 = reduce_send(rb, y, gb, y_peer, part1)
    ring_poll(1)
    ring_poll(2)
    for d, sem_a, sem_b in oth_w:
        arrive(sem_a, o_oth.at[lane_a, :, around(y, -d)])
        arrive(sem_b, o_oth.at[lane_b, around(x, -d)])
    unpack(o_oth, t1)
    t_sib1 = send(t1, t3, sibling)
    ring_poll(3)
    arrive(pa_sib, pa.at[2])
    arrive(pa_fwd, pa.at[3])
    arrive(t_sib0, t2)

    def collect(r, at, g, groups, blocks):
        for sems, part in groups:
            for d, sem in sems:
                arrive(sem, g.at[d - 1, part])
        return [
            r[at, j].astype(F32) + g[0, j].astype(F32) + g[1, j].astype(F32) + g[2, j].astype(F32)
            for j in range(blocks)
        ]

    def repack(sums, out):
        for j in range(6):
            for q in range(4):
                rows = slice(8 * q, 8 * q + 8)
                both = jnp.concatenate([sums[j][rows], sums[6 + j][rows]], axis=0)
                out[q, j] = both.astype(BF16)

    whole = pl.ds(0, 6)
    repack(collect(ra, x, ga, [(a1, part0), (a2, part1)], 12), ya)
    a3 = reduce_send(ya, y, ka, y_peer, whole)
    repack(collect(rb, y, gb, [(b1, part0), (b2, part1)], 12), xb)
    b3 = reduce_send(xb, x, kb, x_peer, whole)
    ring_poll(4)
    arrive(t_sib1, t3)
    back({1: t1, 2: t2, 3: t3})

    def total(r, at, g, sems):
        sums = collect(r, at, g, [(sems, whole)], 6)
        return [jnp.concatenate(sums[3 * q : 3 * q + 3], axis=1).astype(BF16) for q in range(2)]

    stacked = jnp.concatenate(total(ya, y, ka, a3) + total(xb, x, kb, b3), axis=0)
    order = select_rows(
        64,
        64,
        lambda r: lax.div(lax.rem(r, 16), 8) * 32
        + lax.rem(lax.div(r, 2), 2) * 16
        + lax.rem(lax.div(r, 4), 2) * 8
        + lax.div(r, 16) * 2
        + lax.rem(r, 2),
    )
    zs[...] = dot(order, stacked, ((1,), (0,))).astype(BF16).reshape(4, 16, PIECE)
    z_last = []
    for d in (3, 2, 1):
        to = around(z, d)
        z_last.append((d, send(zs.at[to], zr.at[d - 1], device(z=to))))
    ring_poll(5)

    def down(s):
        lanes = slice(s * BLK, (s + 1) * BLK)
        pick = select_rows(64, BLK, lambda r: r + dp * 64)
        mine = dot(pick, act[:, :, lanes].reshape(512, BLK), ((1,), (1,))).astype(BF16)

        def one(k, carry):
            b = col_ref[k, 2 * mp + s]
            seen = jnp.concatenate([tokens(t, b) for t in (t0, t1, t2, t3)], axis=0)
            start = pl.multiple_of(k * BLK, BLK)
            dng_ref[s, :, pl.ds(start, BLK)] = dot(mine, seen, ((1,), (0,))).astype(BF16)
            return carry

        lax.fori_loop(0, KEPT, one, 0)

    down(0)
    ring_poll(6)
    down(1)

    for d, sem in z_last:
        arrive(sem, zr.at[d - 1])
    normed_grad = (
        zs[z].astype(F32) + zr[0].astype(F32) + zr[1].astype(F32) + zr[2].astype(F32)
    )
    scaled = normed_grad * gain16[...]
    unit_rows = unit16[...]
    pack[...] = inv16[:, 0:1] * (
        scaled - token_mean(scaled) - unit_rows * token_mean(scaled * unit_rows)
    )
    for p in range(PIECES):
        gin_ref[:, p * PIECE : (p + 1) * PIECE] = pack[2 * p : 2 * p + 2, :].astype(BF16)

    def z_order(r):
        at = lax.div(r, 32)
        near = lax.rem(lax.div(at, 4) + h, 2)
        return near * 128 + lax.div(lax.rem(r, 32), 2) * 8 + lax.rem(at, 4) * 2 + lax.rem(r, 2)

    order = select_rows(256, 256, z_order)
    for core in range(2):
        both = pg[2 * core : 2 * core + 2].reshape(256, 2 * BLK)
        pg_z[core] = dot(order, both, ((1,), (0,))).astype(BF16)

    for at, sem in nm_sib:
        arrive(sem, n_sib.at[at])

    for s in range(SLOTS):
        lanes = slice(s * BLK, (s + 1) * BLK)

        def grow_up(k, carry):
            b = row_ref[dp * 4 + k, 2 * mp + s]
            picked = jnp.concatenate(
                [
                    jnp.concatenate([n[:, 2 * b], n[:, 2 * b + 1]], axis=-1).reshape(BLK, BLK)
                    for n in (n_own, n_sib)
                ],
                axis=0,
            )
            grads = pg_z[:, :, lanes].reshape(512, BLK)
            start = pl.multiple_of(k * BLK, BLK)
            upg_ref[s, pl.ds(start, BLK), :] = dot(picked, grads, ((0,), (0,))).astype(BF16)
            return carry

        lax.fori_loop(0, 4, grow_up, 0)

    for copy in started:
        copy.wait_send()


def local(
    inputs, out_grad, pre_act, norm_gain, up_weight, down_weight, row_blocks, col_blocks, counts
):
    vmem = pl.BlockSpec(memory_space=pltpu.VMEM)
    smem = pl.BlockSpec(memory_space=pltpu.SMEM)
    hbm = pl.BlockSpec(memory_space=pltpu.HBM)
    return pl.pallas_call(
        kernel,
        out_shape=(
            jax.ShapeDtypeStruct((2, FEATURES), BF16),
            jax.ShapeDtypeStruct((SLOTS, 1024, BLK), BF16),
            jax.ShapeDtypeStruct((SLOTS, 64, 4096), BF16),
        ),
        in_specs=[hbm, hbm, hbm, hbm, hbm, hbm, smem, smem, smem],
        out_specs=(vmem, vmem, vmem),
        scratch_shapes=[
            pltpu.VMEM((2, FEATURES), BF16),
            pltpu.VMEM((2, FEATURES), BF16),
            pltpu.VMEM((1, FEATURES), F32),
            pltpu.VMEM((SLOTS, KEPT + 1, BLK, BLK), BF16),
            pltpu.VMEM((SLOTS, BLK, 4096), BF16),
            pltpu.VMEM((128, 512), BF16),
            pltpu.VMEM((4, 128, 512), BF16),
            pltpu.VMEM((16, PIECE), F32),
            pltpu.VMEM((16, PIECE), F32),
            pltpu.VMEM((16, PIECE), F32),
            pltpu.VMEM((16, 128), F32),
            pltpu.VMEM((4, 16, PIECE), BF16),
            pltpu.VMEM((4, 16, PIECE), BF16),
            pltpu.VMEM((4, 4, 16, PIECE), BF16),
        ]
        + [pltpu.VMEM((LANES, 4, 4, 16, 128), BF16)] * 2
        + [pltpu.VMEM((2 * LANES, 128, 128), BF16)] * 4
        + [pltpu.VMEM((8, 2 * LANES, 32, 128), BF16)] * 2
        + [
            pltpu.VMEM((SLOTS, 384, BLK), F32),
            pltpu.VMEM((4, 128, 512), BF16),
            pltpu.VMEM((4, 128, 512), BF16),
            pltpu.VMEM((2, 256, 512), BF16),
            pltpu.VMEM((128, 512), BF16),
        ]
        + [pltpu.VMEM((4, 12, 32, BLK), BF16)] * 2
        + [pltpu.VMEM((3, 12, 32, BLK), BF16)] * 2
        + [pltpu.VMEM((4, 6, 16, BLK), BF16)] * 2
        + [pltpu.VMEM((3, 6, 16, BLK), BF16)] * 2
        + [
            pltpu.VMEM((4, 16, PIECE), BF16),
            pltpu.VMEM((3, 16, PIECE), BF16),
            pltpu.SMEM((48,), jnp.int32),
            pltpu.SemaphoreType.DMA((7,)),
            pltpu.SemaphoreType.DMA((N_COPIES,)),
            pltpu.SemaphoreType.DMA((N_COPIES,)),
        ],
        compiler_params=pltpu.CompilerParams(
            collective_id=0, has_side_effects=True, vmem_limit_bytes=48 * 1024 * 1024
        ),
    )(
        inputs,
        out_grad,
        pre_act,
        norm_gain.reshape(1, FEATURES),
        up_weight.reshape(SLOTS, KEPT, BLK, BLK),
        down_weight,
        row_blocks.T,
        col_blocks.T,
        counts,
    )


def solution(mesh):
    placed = (
        P(("dp", "mp"), None),
        P(("dp", "mp"), None),
        P("dp", "mp"),
        P(),
        P("mp", None, None),
        P("mp", None, None),
        P(),
        P(),
        P(),
    )
    return jax.shard_map(
        local,
        mesh=mesh,
        in_specs=placed,
        out_specs=(P(("dp", "mp"), None), P("mp", "dp", None), P("mp", "dp", None)),
        check_vma=False,
    )
```

time: 93.4 us -> 78 us (0.84)
  the two profiles are of different devices: /device:TPU:2 before, /device:TPU:6 now
where the time goes in v2:
time: 78 us; the launch traced here: 77.6 us
  Pallas kernels  69.3 us (89%)
  local copies, waits for them, and re-layouts  7.7 us (10%)
    pallas_call x1, Pallas kernels, local(): pl.pallas_call(kernel, out_shape=(jax.ShapeDtypeStruct((2, FEATURES), BF1...  69.3 us
    unnamed x17, local copies, waits for them, and re-layouts  7.7 us

profile of v2, /device:TPU:6, one launch (start us, length us, event | category | flops | bytes accessed | tf_op | source)
XLA Modules:
  0.0 77.6 jit_solution(17343307972322187418)
XLA Ops:
  0.6 0.0 copy-start
  0.6 0.9 %copy-done = bf16[128,512]{1,0:T(8,128)(2,1)S(1)} copy-done((bf16[128,512]{1,0:T(8,128)(2,1)S(1)}, bf16[128,512]{1,0:T(8,128)(2,1)}, u32[]{:S(2)}) %copy-start) | copy-done | bytes 131096
  1.5 0.0 copy-start.1
  1.5 0.7 copy-done.1
  2.3 0.0 copy-start.2
  2.3 0.7 copy-done.2
  3.0 0.0 copy-start.3
  3.0 0.7 copy-done.3
  3.8 0.0 copy-start.4
  3.8 0.7 copy-done.4
  4.5 0.0 copy-start.5
  4.5 0.7 copy-done.5
  5.1 0.0 copy-start.6
  5.1 0.7 copy-done.6
  5.8 69.3 %shard_map.112 = (bf16[2,6144]{1,0:T(2,128)(2,1)S(1)}, bf16[2,1024,256]{2,1,0:T(8,128)(2,1)S(1)}, bf16[2,64,4096]{2,1,0:T(8,128)(2,1)S(1)}) custom-call(bf16[2,6144]{1,0:T(2,128)(2,1)S(1)} %copy-done.1, bf16[2,6144]{1,0:T(2,128)(2,1)S(1)} %copy-done.2, bf16[128,512]{1,0:T(8,128)(2,1)S(1)} %copy-done, f32[1,6144]{1,0:T(1,128)S(1)} %bitcast.4, ...), custom_call_target="tpu_custom_call" | custom-call | tf_op jit(solution)/shard_map/pallas_call | solution.py:494
  75.1 0.6 copy.15
  75.7 1.0 %copy.16 = bf16[2,1024,256]{2,1,0:T(8,128)(2,1)} copy(bf16[2,1024,256]{2,1,0:T(8,128)(2,1)S(1)} %get-tuple-element.7) | data formatting | bytes 2097152
  76.7 1.0 %copy.17 = bf16[2,64,4096]{2,1,0:T(8,128)(2,1)} copy(bf16[2,64,4096]{2,1,0:T(8,128)(2,1)S(1)} %get-tuple-element.8) | data formatting | bytes 2097152
Async XLA Ops:
  0.6 0.9 %copy-start = (bf16[128,512]{1,0:T(8,128)(2,1)S(1)}, bf16[128,512]{1,0:T(8,128)(2,1)}, u32[]{:S(2)}) copy-start(bf16[128,512]{1,0:T(8,128)(2,1)} %pre_hbm.1) | copy-start | bytes 393220
  1.5 0.7 copy-start.1
  2.3 0.7 copy-start.2
  3.0 0.7 copy-start.3
  3.8 0.7 copy-start.4
  4.5 0.7 copy-start.5
  5.1 0.7 copy-start.6

commit v3 on v2

--- a/solution.py
+++ b/solution.py
@@ -145,17 +145,9 @@
     own_z = [
         (d, send(raw_own.at[z], raw_own.at[z], device(z=around(z, d)))) for d in (1, 2, 3)
     ]
-    nm_x = [(d, send(raw_nm.at[y, x], raw_nm.at[y, x], x_peer[d])) for d in (1, 2, 3)]
-    oth_z = [
-        (d, send(raw_own.at[z], raw_oth.at[z], device(h=1 - h, z=around(z, d)))) for d in range(4)
-    ]
-
-    pre_copy.wait()
-    order = select_rows(
-        128, 128, lambda r: lax.div(lax.rem(r, 8), 2) * 32 + lax.div(r, 8) * 2 + lax.rem(r, 2)
-    )
-    pa[0] = dot(order, pre[...], ((1,), (0,))).astype(BF16)
-    pa_sib = send(pa.at[0], pa.at[2], sibling)
+    cut_a, cut_b = pl.ds(0, PIECE // 2), pl.ds(PIECE // 2, PIECE // 2)
+    a, b = raw_nm.at[y, x, :, cut_a], raw_nm.at[y, x, :, cut_b]
+    nm_1 = [(d, send(a, a, x_peer[d]), send(b, b, y_peer[d])) for d in (1, 3, 2)]
 
     def place(raw, tiles, arrivals):
         for d, sem in arrivals:
@@ -191,18 +183,42 @@
     place(raw_own, o_own, own_z)
     own_n = narrow_send(o_own)
     own_w = [(0, column_send(o_own, x, y))]
+    oth_z = [
+        (d, send(raw_own.at[z], raw_oth.at[z], device(h=1 - h, z=around(z, d)))) for d in range(4)
+    ]
+    for d, sem_a, sem_b in nm_1:
+        arrive(sem_a, raw_nm.at[y, around(x, -d), :, cut_a])
+        arrive(sem_b, raw_nm.at[around(y, -d), x, :, cut_b])
+    a, b = raw_nm.at[y, :, :, cut_a], raw_nm.at[:, x, :, cut_b]
+    nm_2 = [(d, send(a, a, y_peer[d]), send(b, b, x_peer[d])) for d in (1, 3, 2)]
+
+    pre_copy.wait()
+    order = select_rows(
+        128, 128, lambda r: lax.div(lax.rem(r, 8), 2) * 32 + lax.div(r, 8) * 2 + lax.rem(r, 2)
+    )
+    pa[0] = dot(order, pre[...], ((1,), (0,))).astype(BF16)
     pa_part = send(pa.at[0], pa.at[1], partner)
-    for d, sem in nm_x:
-        arrive(sem, raw_nm.at[y, around(x, -d)])
-    nm_y = [(d, send(raw_nm.at[y], raw_nm.at[y], y_peer[d])) for d in (1, 2, 3)]
-    place(raw_oth, o_oth, oth_z)
+    pa_sib = send(pa.at[0], pa.at[2], sibling)
+
+    for s in range(SLOTS):
+        up[s, KEPT] = jnp.zeros((BLK, BLK), BF16)
+
+    def locate(b, carry):
+        for s in range(SLOTS):
+            found = jnp.int32(KEPT)
+            for k in range(KEPT):
+                found = jnp.where(row_ref[k, 2 * mp + s] == b, k, found)
+            pos[s * 24 + b] = found
+        return carry
+
+    lax.fori_loop(0, 24, locate, 0)
     for sem in own_n:
         narrow_wait(o_own, sem)
         own_w.append((sem[0], column_send(o_own, around(x, -sem[0]), around(y, -sem[0]))))
-    oth_n = narrow_send(o_oth)
-
-    for d, sem in nm_y:
-        arrive(sem, raw_nm.at[around(y, -d)])
+
+    for d, sem_a, sem_b in nm_2:
+        arrive(sem_a, raw_nm.at[around(y, -d), :, :, cut_a])
+        arrive(sem_b, raw_nm.at[:, around(x, -d), :, cut_b])
     order = select_rows(
         256,
         256,
@@ -247,31 +263,38 @@
     ring_send(1)
     to_sibling(z8)
 
-    for s in range(SLOTS):
-        up[s, KEPT] = jnp.zeros((BLK, BLK), BF16)
-
-    def locate(b, carry):
-        for s in range(SLOTS):
-            found = jnp.int32(KEPT)
-            for k in range(KEPT):
-                found = jnp.where(row_ref[k, 2 * mp + s] == b, k, found)
-            pos[s * 24 + b] = found
-        return carry
-
-    lax.fori_loop(0, 24, locate, 0)
-    for sem in oth_n:
-        narrow_wait(o_oth, sem)
-    arrive(pa_part, pa.at[1])
-    pa_fwd = send(pa.at[1], pa.at[3], sibling)
+    place(raw_oth, o_oth, oth_z)
+    oth_n = narrow_send(o_oth)
     for copy in weight_copies:
         copy.wait()
-    ring_poll(0)
     for far, sems in own_w:
         for d, sem_a, sem_b in sems:
             arrive(sem_a, o_own.at[lane_a, around(x, -far), around(y, -d)])
             arrive(sem_b, o_own.at[lane_b, around(x, -d), around(y, -far)])
-    a, b = o_oth.at[lane_a, :, y], o_oth.at[lane_b, x]
-    oth_w = [(d, send(a, a, y_peer[d]), send(b, b, x_peer[d])) for d in (1, 3, 2)]
+    for sem in oth_n:
+        narrow_wait(o_oth, sem)
+
+    def wide_send(o, lanes_a, lanes_b, from_x, from_y, d):
+        a, b = o.at[lanes_a, :, from_y], o.at[lanes_b, from_x]
+        return send(a, a, y_peer[d]), send(b, b, x_peer[d])
+
+    def wide_wait(o, lanes_a, lanes_b, sems, d):
+        arrive(sems[0], o.at[lanes_a, :, around(y, -d)])
+        arrive(sems[1], o.at[lanes_b, around(x, -d)])
+
+    quarter = [pl.ds(6 * k, 6) for k in range(4)]
+    oth_w = {d: wide_send(o_oth, lane_a, lane_b, x, y, d) for d in (1, 3)}
+
+    def oth_relay():
+        for d, qa, qb in ((1, quarter[0], quarter[2]), (3, quarter[1], quarter[3])):
+            wide_wait(o_oth, lane_a, lane_b, oth_w[d], d)
+            oth_w[d + 10] = wide_send(o_oth, qa, qb, around(x, -d), around(y, -d), d)
+
+    def oth_finish():
+        wide_wait(o_oth, quarter[0], quarter[2], oth_w[11], 2)
+        wide_wait(o_oth, quarter[1], quarter[3], oth_w[13], 2)
+
+    ring_poll(0)
 
     def unpack(o, t):
         def one(k, carry):
@@ -290,7 +313,7 @@
     def tokens(t, b):
         return jnp.concatenate([t[2 * b], t[2 * b + 1]], axis=-1)
 
-    def back(groups):
+    def back(groups, between=lambda: None):
         rows = 128 * len(groups)
         for s in range(SLOTS):
 
@@ -315,6 +338,8 @@
                 return carry
 
             lax.fori_loop(0, KEPT // 4, grow, 0)
+            if s == 0:
+                between()
 
         def derive(j, carry):
             at = pl.ds(pl.multiple_of(j * 16, 16), 16)
@@ -329,7 +354,7 @@
 
         lax.fori_loop(0, 8, derive, 0)
 
-    back({0: t0})
+    back({0: t0}, lambda: ring_poll(1))
 
     order = select_rows(
         128, 128, lambda r: lax.div(lax.rem(r, 32), 8) * 32 + lax.div(r, 32) * 8 + lax.rem(r, 8)
@@ -360,17 +385,17 @@
     a2 = reduce_send(ra, x, ga, x_peer, part1)
     terms(pgb[...], rb, 12, 6)
     b2 = reduce_send(rb, y, gb, y_peer, part1)
-    ring_poll(1)
+    oth_relay()
     ring_poll(2)
-    for d, sem_a, sem_b in oth_w:
-        arrive(sem_a, o_oth.at[lane_a, :, around(y, -d)])
-        arrive(sem_b, o_oth.at[lane_b, around(x, -d)])
+    arrive(pa_part, pa.at[1])
+    pa_fwd = send(pa.at[1], pa.at[3], sibling)
+    arrive(pa_sib, pa.at[2])
+    arrive(t_sib0, t2)
+    back({2: t2})
+    ring_poll(3)
+    oth_finish()
     unpack(o_oth, t1)
     t_sib1 = send(t1, t3, sibling)
-    ring_poll(3)
-    arrive(pa_sib, pa.at[2])
-    arrive(pa_fwd, pa.at[3])
-    arrive(t_sib0, t2)
 
     def collect(r, at, g, groups, blocks):
         for sems, part in groups:
@@ -393,9 +418,9 @@
     a3 = reduce_send(ya, y, ka, y_peer, whole)
     repack(collect(rb, y, gb, [(b1, part0), (b2, part1)], 12), xb)
     b3 = reduce_send(xb, x, kb, x_peer, whole)
-    ring_poll(4)
+    arrive(pa_fwd, pa.at[3])
     arrive(t_sib1, t3)
-    back({1: t1, 2: t2, 3: t3})
+    back({1: t1, 3: t3}, lambda: ring_poll(4))
 
     def total(r, at, g, sems):
         sums = collect(r, at, g, [(sems, whole)], 6)
@@ -433,8 +458,8 @@
         lax.fori_loop(0, KEPT, one, 0)
 
     down(0)
+    down(1)
     ring_poll(6)
-    down(1)
 
     for d, sem in z_last:
         arrive(sem, zr.at[d - 1])
@@ -494,9 +519,9 @@
     return pl.pallas_call(
         kernel,
         out_shape=(
-            jax.ShapeDtypeStruct((2, FEATURES), BF16),
-            jax.ShapeDtypeStruct((SLOTS, 1024, BLK), BF16),
-            jax.ShapeDtypeStruct((SLOTS, 64, 4096), BF16),
+            pltpu.VMEM((2, FEATURES), BF16),
+            pltpu.VMEM((SLOTS, 1024, BLK), BF16),
+            pltpu.VMEM((SLOTS, 64, 4096), BF16),
         ),
         in_specs=[hbm, hbm, hbm, hbm, hbm, hbm, smem, smem, smem],
         out_specs=(vmem, vmem, vmem),
@@ -539,7 +564,7 @@
             pltpu.SemaphoreType.DMA((N_COPIES,)),
         ],
         compiler_params=pltpu.CompilerParams(
-            collective_id=0, has_side_effects=True, vmem_limit_bytes=48 * 1024 * 1024
+            collective_id=0, has_side_effects=True, vmem_limit_bytes=56 * 1024 * 1024
         ),
     )(
         inputs,

time: 78 us -> 72.5 us (0.929)
  the two profiles are of different devices: /device:TPU:6 before, /device:TPU:1 now
where the time goes in v3:
time: 72.5 us; the launch traced here: 72.4 us
  Pallas kernels  69.2 us (95%)
  local copies, waits for them, and re-layouts  2.55 us (4%)
    pallas_call x1, Pallas kernels, local(): pl.pallas_call(kernel, out_shape=(pltpu.VMEM((2, FEATURES), BF16), pltpu....  69.2 us
    unnamed x3, local copies, waits for them, and re-layouts  2.55 us

profile of v3, /device:TPU:1, one launch (start us, length us, event | category | flops | bytes accessed | tf_op | source)
XLA Modules:
  0.0 72.4 jit_solution(13012760379904220153)
XLA Ops:
  0.6 69.2 %shard_map.112 = (bf16[2,6144]{1,0:T(2,128)(2,1)S(1)}, bf16[2,1024,256]{2,1,0:T(8,128)(2,1)S(1)}, bf16[2,64,4096]{2,1,0:T(8,128)(2,1)S(1)}) custom-call(bf16[2,6144]{1,0:T(2,128)(2,1)} %x_hbm.1, bf16[2,6144]{1,0:T(2,128)(2,1)} %og_hbm.1, bf16[128,512]{1,0:T(8,128)(2,1)} %pre_hbm.1, f32[1,6144]{1,0:T(1,128)} %bitcast.5, bf16[2,16,256,256]{3,2,1,0:T(8,128)(2,1)} %bitcast.4, ...), custom_call_target="tpu_custom_call" | custom-call | tf_op jit(solution)/shard_map/pallas_call | solution.py:519
  69.8 0.6 copy.15
  70.4 1.0 %copy.16 = bf16[2,1024,256]{2,1,0:T(8,128)(2,1)} copy(bf16[2,1024,256]{2,1,0:T(8,128)(2,1)S(1)} %get-tuple-element.4) | data formatting | bytes 2097152
  71.4 1.0 %copy.17 = bf16[2,64,4096]{2,1,0:T(8,128)(2,1)} copy(bf16[2,64,4096]{2,1,0:T(8,128)(2,1)S(1)} %get-tuple-element.5) | data formatting | bytes 2097152

commit v4 on v3

--- a/solution.py
+++ b/solution.py
@@ -303,7 +303,7 @@
             t[LANES + k] = rows[:, 1].reshape(128, 128).astype(BF16)
             return carry
 
-        lax.fori_loop(0, LANES, one, 0)
+        lax.fori_loop(0, LANES, one, 0, unroll=4)
 
     unpack(o_own, t0)
     t_sib0 = send(t0, t2, sibling)
@@ -316,6 +316,7 @@
     def back(groups, between=lambda: None):
         rows = 128 * len(groups)
         for s in range(SLOTS):
+            acc[s, 0:rows] = jnp.zeros((rows, BLK), F32)
 
             def grow(k, carry):
                 parts = []
@@ -327,17 +328,10 @@
                     jnp.concatenate(parts, axis=1), dn[s, :, pl.ds(start, 1024)], ((1,), (1,))
                 )
 
-                @pl.when(k == 0)
-                def _():
-                    acc[s, 0:rows] = term
-
-                @pl.when(k > 0)
-                def _():
-                    acc[s, 0:rows] += term
-
+                acc[s, 0:rows] += term
                 return carry
 
-            lax.fori_loop(0, KEPT // 4, grow, 0)
+            lax.fori_loop(0, KEPT // 4, grow, 0, unroll=True)
             if s == 0:
                 between()
 
@@ -352,7 +346,7 @@
                     act[g, at, lanes] = jnp.where(live[s], value, 0.0).astype(BF16)
             return carry
 
-        lax.fori_loop(0, 8, derive, 0)
+        lax.fori_loop(0, 8, derive, 0, unroll=4)
 
     back({0: t0}, lambda: ring_poll(1))
 
@@ -369,7 +363,7 @@
                 out[q, b] = term[32 * q : 32 * q + 32]
             return carry
 
-        lax.fori_loop(first, first + 6, one, 0)
+        lax.fori_loop(first, first + 6, one, 0, unroll=True)
 
     def reduce_send(r, at, g, peers, blocks):
         return [
@@ -455,7 +449,7 @@
             dng_ref[s, :, pl.ds(start, BLK)] = dot(mine, seen, ((1,), (0,))).astype(BF16)
             return carry
 
-        lax.fori_loop(0, KEPT, one, 0)
+        lax.fori_loop(0, KEPT, one, 0, unroll=8)
 
     down(0)
     down(1)
@@ -504,7 +498,7 @@
             upg_ref[s, pl.ds(start, BLK), :] = dot(picked, grads, ((0,), (0,))).astype(BF16)
             return carry
 
-        lax.fori_loop(0, 4, grow_up, 0)
+        lax.fori_loop(0, 4, grow_up, 0, unroll=True)
 
     for copy in started:
         copy.wait_send()

time: 72.5 us -> 67.7 us (0.934)
  Pallas kernels: 69.2 us -> 64.3 us
    pallas_call x1, Pallas kernels: 69.2 us -> 64.3 us  [local(): pl.pallas_call(kernel, out_shape=(pltpu.VMEM((2, FEATURES), BF16), pltpu....]
where the time goes in v4:
time: 67.7 us; the launch traced here: 67.5 us
  Pallas kernels  64.3 us (95%)
  local copies, waits for them, and re-layouts  2.55 us (4%)
    pallas_call x1, Pallas kernels, local(): pl.pallas_call(kernel, out_shape=(pltpu.VMEM((2, FEATURES), BF16), pltpu....  64.3 us
    unnamed x3, local copies, waits for them, and re-layouts  2.55 us

profile of v4, /device:TPU:1, one launch (start us, length us, event | category | flops | bytes accessed | tf_op | source)
XLA Modules:
  0.0 67.5 jit_solution(7138118757908576262)
XLA Ops:
  0.6 64.3 %shard_map.112 = (bf16[2,6144]{1,0:T(2,128)(2,1)S(1)}, bf16[2,1024,256]{2,1,0:T(8,128)(2,1)S(1)}, bf16[2,64,4096]{2,1,0:T(8,128)(2,1)S(1)}) custom-call(bf16[2,6144]{1,0:T(2,128)(2,1)} %x_hbm.1, bf16[2,6144]{1,0:T(2,128)(2,1)} %og_hbm.1, bf16[128,512]{1,0:T(8,128)(2,1)} %pre_hbm.1, f32[1,6144]{1,0:T(1,128)} %bitcast.5, bf16[2,16,256,256]{3,2,1,0:T(8,128)(2,1)} %bitcast.4, ...), custom_call_target="tpu_custom_call" | custom-call | tf_op jit(solution)/shard_map/pallas_call | solution.py:513
  65.0 0.6 copy.15
  65.6 1.0 %copy.16 = bf16[2,1024,256]{2,1,0:T(8,128)(2,1)} copy(bf16[2,1024,256]{2,1,0:T(8,128)(2,1)S(1)} %get-tuple-element.4) | data formatting | bytes 2097152
  66.6 1.0 %copy.17 = bf16[2,64,4096]{2,1,0:T(8,128)(2,1)} copy(bf16[2,64,4096]{2,1,0:T(8,128)(2,1)S(1)} %get-tuple-element.5) | data formatting | bytes 2097152

commit v5 on v4

--- a/solution.py
+++ b/solution.py
@@ -46,7 +46,7 @@
     pack, gain16, unit16, inv16,
     raw_own, raw_oth, raw_nm,
     o_own, o_oth, t0, t1, t2, t3, n_own, n_sib,
-    acc, act, pg, pg_z, pgb,
+    acc, act, pg, pg_z, pgb, up_own,
     ra, rb, ga, gb, ya, xb, ka, kb,
     zs, zr, pos,
     local_sem, send_sem, recv_sem,
@@ -478,30 +478,43 @@
         both = pg[2 * core : 2 * core + 2].reshape(256, 2 * BLK)
         pg_z[core] = dot(order, both, ((1,), (0,))).astype(BF16)
 
+    def up_part(n, core, store):
+        for s in range(SLOTS):
+            grads = pg_z[core, :, s * BLK : (s + 1) * BLK]
+
+            def one(k, carry):
+                b = row_ref[dp * 4 + k, 2 * mp + s]
+                picked = jnp.concatenate([n[:, 2 * b], n[:, 2 * b + 1]], axis=-1)
+                store(s, k, dot(picked.reshape(BLK, BLK), grads, ((0,), (0,))))
+                return carry
+
+            lax.fori_loop(0, 4, one, 0, unroll=True)
+
+    def keep(s, k, part):
+        up_own[s, k] = part
+
+    def finish_up(s, k, part):
+        start = pl.multiple_of(k * BLK, BLK)
+        upg_ref[s, pl.ds(start, BLK), :] = (up_own[s, k] + part).astype(BF16)
+
+    up_part(n_own, 0, keep)
     for at, sem in nm_sib:
         arrive(sem, n_sib.at[at])
-
-    for s in range(SLOTS):
-        lanes = slice(s * BLK, (s + 1) * BLK)
-
-        def grow_up(k, carry):
-            b = row_ref[dp * 4 + k, 2 * mp + s]
-            picked = jnp.concatenate(
-                [
-                    jnp.concatenate([n[:, 2 * b], n[:, 2 * b + 1]], axis=-1).reshape(BLK, BLK)
-                    for n in (n_own, n_sib)
-                ],
-                axis=0,
-            )
-            grads = pg_z[:, :, lanes].reshape(512, BLK)
-            start = pl.multiple_of(k * BLK, BLK)
-            upg_ref[s, pl.ds(start, BLK), :] = dot(picked, grads, ((0,), (0,))).astype(BF16)
-            return carry
-
-        lax.fori_loop(0, 4, grow_up, 0, unroll=True)
+    up_part(n_sib, 1, finish_up)
 
     for copy in started:
         copy.wait_send()
+
+
+def write_out(a, b, c, a_out, b_out, c_out, sem):
+    copies = [
+        pltpu.make_async_copy(src, dst, sem.at[k])
+        for k, (src, dst) in enumerate([(a, a_out), (b, b_out), (c, c_out)])
+    ]
+    for copy in copies:
+        copy.start()
+    for copy in copies:
+        copy.wait()
 
 
 def local(
@@ -510,7 +523,7 @@
     vmem = pl.BlockSpec(memory_space=pltpu.VMEM)
     smem = pl.BlockSpec(memory_space=pltpu.SMEM)
     hbm = pl.BlockSpec(memory_space=pltpu.HBM)
-    return pl.pallas_call(
+    results = pl.pallas_call(
         kernel,
         out_shape=(
             pltpu.VMEM((2, FEATURES), BF16),
@@ -544,6 +557,7 @@
             pltpu.VMEM((4, 128, 512), BF16),
             pltpu.VMEM((2, 256, 512), BF16),
             pltpu.VMEM((128, 512), BF16),
+            pltpu.VMEM((SLOTS, 4, BLK, BLK), F32),
         ]
         + [pltpu.VMEM((4, 12, 32, BLK), BF16)] * 2
         + [pltpu.VMEM((3, 12, 32, BLK), BF16)] * 2
@@ -571,6 +585,14 @@
         col_blocks.T,
         counts,
     )
+    return pl.pallas_call(
+        write_out,
+        out_shape=[jax.ShapeDtypeStruct(r.shape, r.dtype) for r in results],
+        in_specs=[vmem] * 3,
+        out_specs=[hbm] * 3,
+        scratch_shapes=[pltpu.SemaphoreType.DMA((3,))],
+        compiler_params=pltpu.CompilerParams(vmem_limit_bytes=8 * 1024 * 1024),
+    )(*results)
 
 
 def solution(mesh):

time: 67.7 us -> 66.4 us (0.981)
  local copies, waits for them, and re-layouts: 2.55 us -> 0 us
  Pallas kernels: 64.3 us -> 65.7 us
    unnamed x3 -> x0, local copies, waits for them, and re-layouts: 2.55 us -> none
    pallas_call x0 -> x1, Pallas kernels: none -> 1.35 us  [local(): pl.pallas_call(write_out, out_shape=[jax.ShapeDtypeStruct(r.shape, r.dtyp...]
where the time goes in v5:
time: 66.4 us; the launch traced here: 66.3 us
  Pallas kernels  65.7 us (99%)
    pallas_call x1, Pallas kernels, local(): pl.pallas_call(kernel, out_shape=(pltpu.VMEM((2, FEATURES), BF16), pltpu....  64.3 us
    pallas_call x1, Pallas kernels, local(): pl.pallas_call(write_out, out_shape=[jax.ShapeDtypeStruct(r.shape, r.dtyp...  1.35 us

profile of v5, /device:TPU:1, one launch (start us, length us, event | category | flops | bytes accessed | tf_op | source)
XLA Modules:
  0.0 66.3 jit_solution(7465898814686278298)
XLA Ops:
  0.6 64.3 %shard_map.112 = (bf16[2,6144]{1,0:T(2,128)(2,1)S(1)}, bf16[2,1024,256]{2,1,0:T(8,128)(2,1)S(1)}, bf16[2,64,4096]{2,1,0:T(8,128)(2,1)S(1)}) custom-call(bf16[2,6144]{1,0:T(2,128)(2,1)} %x_hbm.1, bf16[2,6144]{1,0:T(2,128)(2,1)} %og_hbm.1, bf16[128,512]{1,0:T(8,128)(2,1)} %pre_hbm.1, f32[1,6144]{1,0:T(1,128)} %bitcast.5, bf16[2,16,256,256]{3,2,1,0:T(8,128)(2,1)} %bitcast.4, ...), custom_call_target="tpu_custom_call" | custom-call | tf_op jit(solution)/shard_map/pallas_call | solution.py:526
  64.9 1.4 %shard_map.113 = (bf16[2,6144]{1,0:T(2,128)(2,1)}, bf16[2,1024,256]{2,1,0:T(8,128)(2,1)}, bf16[2,64,4096]{2,1,0:T(8,128)(2,1)}) custom-call(bf16[2,6144]{1,0:T(2,128)(2,1)S(1)} %get-tuple-element.6.a, bf16[2,1024,256]{2,1,0:T(8,128)(2,1)S(1)} %get-tuple-element.7.b, bf16[2,64,4096]{2,1,0:T(8,128)(2,1)S(1)} %get-tuple-element.8.c), custom_call_target="tpu_custom_call" | custom-call | tf_op jit(solution)/shard_map/pallas_call | solution.py:588

commit v6 on v5

--- a/solution.py
+++ b/solution.py
@@ -282,17 +282,11 @@
         arrive(sems[0], o.at[lanes_a, :, around(y, -d)])
         arrive(sems[1], o.at[lanes_b, around(x, -d)])
 
-    quarter = [pl.ds(6 * k, 6) for k in range(4)]
-    oth_w = {d: wide_send(o_oth, lane_a, lane_b, x, y, d) for d in (1, 3)}
-
-    def oth_relay():
-        for d, qa, qb in ((1, quarter[0], quarter[2]), (3, quarter[1], quarter[3])):
+    oth_w = {d: wide_send(o_oth, lane_a, lane_b, x, y, d) for d in (1, 3, 2)}
+
+    def oth_finish():
+        for d in (1, 3, 2):
             wide_wait(o_oth, lane_a, lane_b, oth_w[d], d)
-            oth_w[d + 10] = wide_send(o_oth, qa, qb, around(x, -d), around(y, -d), d)
-
-    def oth_finish():
-        wide_wait(o_oth, quarter[0], quarter[2], oth_w[11], 2)
-        wide_wait(o_oth, quarter[1], quarter[3], oth_w[13], 2)
 
     ring_poll(0)
 
@@ -367,7 +361,7 @@
 
     def reduce_send(r, at, g, peers, blocks):
         return [
-            (d, send(r.at[around(at, d), blocks], g.at[d - 1, blocks], peers[d])) for d in (2, 1, 3)
+            (d, send(r.at[around(at, d), blocks], g.at[d - 1, blocks], peers[d])) for d in (1, 3, 2)
         ]
 
     part0, part1 = pl.ds(0, 6), pl.ds(6, 6)
@@ -379,7 +373,6 @@
     a2 = reduce_send(ra, x, ga, x_peer, part1)
     terms(pgb[...], rb, 12, 6)
     b2 = reduce_send(rb, y, gb, y_peer, part1)
-    oth_relay()
     ring_poll(2)
     arrive(pa_part, pa.at[1])
     pa_fwd = send(pa.at[1], pa.at[3], sibling)

time: 66.4 us -> 64.1 us (0.965)
  Pallas kernels: 65.7 us -> 63.3 us
    pallas_call x1, Pallas kernels: 64.3 us -> 62 us  [local(): pl.pallas_call(kernel, out_shape=(pltpu.VMEM((2, FEATURES), BF16), pltpu....]
where the time goes in v6:
time: 64.1 us; the launch traced here: 64 us
  Pallas kernels  63.3 us (99%)
    pallas_call x1, Pallas kernels, local(): pl.pallas_call(kernel, out_shape=(pltpu.VMEM((2, FEATURES), BF16), pltpu....  62 us
    pallas_call x1, Pallas kernels, local(): pl.pallas_call(write_out, out_shape=[jax.ShapeDtypeStruct(r.shape, r.dtyp...  1.35 us

profile of v6, /device:TPU:1, one launch (start us, length us, event | category | flops | bytes accessed | tf_op | source)
XLA Modules:
  0.0 64.0 jit_solution(13012420312919554210)
XLA Ops:
  0.6 62.0 %shard_map.112 = (bf16[2,6144]{1,0:T(2,128)(2,1)S(1)}, bf16[2,1024,256]{2,1,0:T(8,128)(2,1)S(1)}, bf16[2,64,4096]{2,1,0:T(8,128)(2,1)S(1)}) custom-call(bf16[2,6144]{1,0:T(2,128)(2,1)} %x_hbm.1, bf16[2,6144]{1,0:T(2,128)(2,1)} %og_hbm.1, bf16[128,512]{1,0:T(8,128)(2,1)} %pre_hbm.1, f32[1,6144]{1,0:T(1,128)} %bitcast.5, bf16[2,16,256,256]{3,2,1,0:T(8,128)(2,1)} %bitcast.4, ...), custom_call_target="tpu_custom_call" | custom-call | tf_op jit(solution)/shard_map/pallas_call | solution.py:519
  62.6 1.4 %shard_map.113 = (bf16[2,6144]{1,0:T(2,128)(2,1)}, bf16[2,1024,256]{2,1,0:T(8,128)(2,1)}, bf16[2,64,4096]{2,1,0:T(8,128)(2,1)}) custom-call(bf16[2,6144]{1,0:T(2,128)(2,1)S(1)} %get-tuple-element.6.a, bf16[2,1024,256]{2,1,0:T(8,128)(2,1)S(1)} %get-tuple-element.7.b, bf16[2,64,4096]{2,1,0:T(8,128)(2,1)S(1)} %get-tuple-element.8.c), custom_call_target="tpu_custom_call" | custom-call | tf_op jit(solution)/shard_map/pallas_call | solution.py:581
